TPU v7x, 32 devices: a whole 2x2x4 slice. The times are simulated.
32 devices in a mesh: dp: 8 (over y, x, core), tensor: 4 (over z).
Axes of the slice: x: 2, y: 2, z: 4, core: 2. Of those that a mesh axis runs over, the one named last changes fastest.
Arguments:
- hidden: bfloat16 [4096, 8192], P(('dp', 'tensor')), may hold values from -50 to 50
- out_weight: bfloat16 [128256, 8192], P(('dp', 'tensor')), may hold values from -1 to 1
- loss_mask: int32 [4096], P(('dp', 'tensor')), may hold values from 0 to 1, as said below
- targets: int32 [4096], P(('dp', 'tensor')), may hold values from 0 to 128255
- kept_count: int32 [32], P(('dp', 'tensor')), may hold values from 0 to 1, as said below
Outputs:
- hidden_grad: bfloat16 [4096, 8192], P(('dp', 'tensor'))
- row_loss: float32 [4096], P(('dp', 'tensor'))
Inputs may be any that keep to these rules, and one draw needn't show every extreme that they name: `loss_mask`: each device's 128 rows hold at least 1 ones. `kept_count`: some entry equals 1 and some entry equals 0.
All inputs are finite; a program needn't handle non-finite values.
Results may differ from a plain program's by a relative error of at most 0.0026.
Values may be sent and summed in bfloat16 or wider, within the bound.
A program may use at most 128 MiB of HBM per device.

v0:
```python
import jax
import jax.numpy as jnp
from jax import lax
from jax.sharding import PartitionSpec as P

CAP = 1


loss_scale = 128.0


def shards(hidden, out_weight, loss_mask, targets, kept_count):
    order_pos = jnp.cumsum(loss_mask) - 1
    kept_row = (loss_mask == 1) & (order_pos < kept_count[0])
    slot_ids = jnp.arange(CAP, dtype=jnp.int32)
    slot_hits = kept_row[None, :] & (order_pos[None, :] == slot_ids[:, None])
    packed = jnp.dot(
        slot_hits.astype(jnp.bfloat16), hidden, preferred_element_type=jnp.float32
    ).astype(jnp.bfloat16)
    slot_target = jnp.sum(jnp.where(slot_hits, targets[None, :], 0), axis=1)
    packed_target = jnp.where(jnp.any(slot_hits, axis=1), slot_target, -1)
    gathered, gathered_target = (
        lax.all_gather(packed, ("dp", "tensor"), axis=0, tiled=True),
        lax.all_gather(packed_target, ("dp", "tensor"), axis=0, tiled=True),
    )
    filled = gathered_target >= 0
    vocab_rows = out_weight.shape[0]
    device_pos = lax.axis_index(("dp", "tensor"))
    vocab_ids = device_pos * vocab_rows + jnp.arange(vocab_rows, dtype=jnp.int32)
    logits = jnp.einsum("rd,vd->rv", gathered, out_weight, preferred_element_type=jnp.float32)
    target_hit = vocab_ids[None, :] == gathered_target[:, None]
    local_top = jnp.max(logits, axis=1)
    local_pick = jnp.sum(jnp.where(target_hit, logits, 0.0), axis=1)
    row_top = lax.pmax(local_top, ("dp", "tensor"))
    shifted_total = jnp.sum(jnp.exp(logits - row_top[:, None]), axis=1)
    row_total, picked = lax.psum((shifted_total, local_pick), ("dp", "tensor"))
    log_total = row_top + jnp.log(row_total)
    slot_loss = jnp.where(filled, log_total - picked, 0.0)
    probabilities = jnp.exp(logits - log_total[:, None])
    coefficient = jnp.where(
        filled[:, None], probabilities - target_hit.astype(jnp.float32), 0.0
    ).astype(jnp.bfloat16)
    dp_count = lax.axis_size("dp")
    tensor_count = lax.axis_size("tensor")
    grad_term = jnp.dot(coefficient, out_weight, preferred_element_type=jnp.float32)
    grad_term = grad_term.reshape(dp_count, tensor_count, CAP, grad_term.shape[1])
    partial_sum = lax.psum_scatter(grad_term, "tensor", scatter_dimension=1, tiled=True)
    own_grad = lax.psum_scatter(partial_sum, "dp", scatter_dimension=0, tiled=True)
    own_grad = own_grad.reshape(CAP, own_grad.shape[3])
    own_grad = own_grad * loss_scale
    own_loss = lax.dynamic_slice_in_dim(slot_loss, device_pos * CAP, CAP, 0)
    slot_pos = jnp.clip(order_pos, 0, CAP - 1)
    hidden_grad = jnp.where(kept_row[:, None], own_grad[slot_pos], 0.0).astype(jnp.bfloat16)
    row_loss = jnp.where(kept_row, own_loss[slot_pos], 0.0)
    return (hidden_grad, row_loss)


def solution(mesh):
    in_specs = (
        P(("dp", "tensor"), None),
        P(("dp", "tensor"), None),
        P(("dp", "tensor")),
        P(("dp", "tensor")),
        P(("dp", "tensor")),
    )
    out_specs = (P(("dp", "tensor"), None), P(("dp", "tensor")))
    return jax.shard_map(shards, mesh=mesh, in_specs=in_specs, out_specs=out_specs, check_vma=False)
```

profile of v0, /device:TPU:0, one launch (start us, length us, event | category | flops | bytes accessed | tf_op | source)
XLA Modules:
  0.0 350.7 jit_solution(1307423571236316626)
XLA Ops:
  7.2 0.0 copy-start
  7.2 0.0 reduce-scatter.3.cloned.1.call-start
  8.0 0.8 copy.9
  8.8 0.2 reduce-window.4
  9.0 0.1 compare_reduce_fusion
  9.1 1.3 select_reduce_fusion
  10.4 0.6 and_reduce_fusion
  12.3 0.1 dynamic-update-slice
  12.5 42.0 %all-reduce = s32[32]{0:T(128)S(1)} all-reduce(s32[32]{0:T(128)S(1)} %dynamic-update-slice), channel_id=1, replica_groups=mesh['dp'=8,'tensor'=4] {'dp','tensor'}, use_global_device_ids=true, to_apply=%add | all-reduce | flops 32 | bytes 256
  54.5 0.0 copy-done
  54.5 0.4 fusion.11
  54.9 70.4 %all-gather = bf16[262144]{0:T(1024)(128)(2,1)S(1)} all-gather(bf16[8192]{0:T(1024)(128)(2,1)S(1)} %convert_element_type.16), channel_id=2, replica_groups=mesh['dp'=8,'tensor'=4] {'dp','tensor'}, dimensions={0}, use_global_device_ids=true | all-gather | bytes 540672 | tf_op jit(solution)/shard_map/all_gather | solution.py:23
  125.3 0.2 reshape.69
  125.6 26.0 %fusion.15 = (f32[32]{0:T(128)S(1)}, f32[32,4008]{1,0:T(8,128)S(1)}) fusion(bf16[32,8192]{1,0:T(8,128)(2,1)S(1)} %reshape.69, bf16[4008,8192]{1,0:T(8,128)(2,1)} %param.6), kind=kOutput, calls=%fused_computation.29 | convolution fusion | flops 2101474560 | bytes 66704512 | tf_op jit(solution)/shard_map/rd,vd->rv/dot_general | solution.py:30
  151.6 37.6 %pmax.7 = f32[32]{0:T(128)S(1)} all-reduce(f32[32]{0:T(128)S(1)} %get-tuple-element.12), channel_id=1, replica_groups=mesh['dp'=8,'tensor'=4] {'dp','tensor'}, use_global_device_ids=true, to_apply=%region_4.5 | all-reduce | flops 32 | bytes 256 | tf_op jit(solution)/shard_map/pmax | solution.py:34
  189.1 0.3 fusion.3
  189.5 41.5 %all-reduce.2 = (f32[32]{0:T(128)S(1)}, f32[32]{0:T(128)S(1)}) all-reduce(f32[32]{0:T(128)S(1)} %get-tuple-element.3, f32[32]{0:T(128)S(1)} %get-tuple-element.2), channel_id=1, replica_groups=mesh['dp'=8,'tensor'=4] {'dp','tensor'}, use_global_device_ids=true, to_apply=%region_6.7 | all-reduce | flops 64 | bytes 512 | tf_op jit(solution)/shard_map/psum | solution.py:36
  231.0 0.0 copy-start.1
  231.0 24.1 %fusion.4 = f32[32,8192]{1,0:T(8,128)} fusion(bf16[4008,8192]{1,0:T(8,128)(2,1)} %param.6, f32[32,4008]{1,0:T(8,128)S(1)} %get-tuple-element.13, s32[4008]{0:T(1024)S(1)} %iota_add_fusion, f32[32]{0:T(128)S(1)} %get-tuple-element.9, s32[32]{0:T(128)S(1)} %all-reduce, pred[32]{0:T(512)(128)(4,1)S(1)} %broadcast_compare_fusion), kind=kOutput, calls=%fused_computation.8 | convolution fusion | flops 2102115840 | bytes 67244992 | tf_op jit(solution)/shard_map/dot_general | solution.py:45
  255.1 0.0 copy-start.2
  255.1 1.5 reshape.66
  256.7 1.6 copy.10
  258.3 0.0 reduce-scatter.3.cloned.1.call-update
  258.3 0.0 all-reduce.5.cloned.1.call-start
  258.3 0.0 copy-done.2
  258.3 0.6 dynamic-slice
  259.0 0.6 dynamic_slice.5
  259.6 25.1 %reduce-scatter.3.cloned.1.call-done = f32[8,1,1,8192]{3,0,2,1:T(8,128)} async-done(((f32[8,4,1,8192]{3,0,2,1:T(8,128)}), f32[8,1,1,8192]{3,0,2,1:T(8,128)}) %reduce-scatter.3.cloned.1.call-update) | async-done | bytes 262160 | tf_op jit(solution)/shard_map/reduce_scatter | solution.py:47
  284.7 1.9 copy.11
  286.6 0.0 all-reduce.5.cloned.1.call-update
  286.6 1.1 broadcast_select_fusion
  287.8 53.0 %all-reduce.5.cloned.1.call-done = f32[8,1,1,8192]{3,1,0,2:T(1,128)} async-done(((f32[8,1,1,8192]{3,1,0,2:T(1,128)}), f32[8,1,1,8192]{3,1,0,2:T(1,128)}) %all-reduce.5.cloned.1.call-update) | async-done | bytes 262160
  340.8 1.4 dynamic-slice_multiply_fusion
  342.2 1.7 select_convert_fusion
  343.9 0.0 copy-done.1
  (5 shorter events, 0.0 us)
Async XLA Ops:
  7.2 47.3 %copy-start = (bf16[128,8192]{1,0:T(8,128)(2,1)S(1)}, bf16[128,8192]{1,0:T(8,128)(2,1)}, u32[]{:S(2)}) copy-start(bf16[128,8192]{1,0:T(8,128)(2,1)} %param.5) | copy-start | bytes 6291460
  7.2 277.5 %reduce-scatter.3.cloned.1.call-start = ((), (), s32[]{:S(2)}) async-start(), calls=%async_computation.1 | async-start | bytes 1310720 | tf_op jit(solution)/shard_map/reduce_scatter | solution.py:47
  231.0 112.9 %copy-start.1 = (bf16[128,8192]{1,0:T(8,128)(2,1)S(1)}, bf16[128,8192]{1,0:T(8,128)(2,1)}, u32[]{:S(2)}) copy-start(bf16[128,8192]{1,0:T(8,128)(2,1)} %param.5) | copy-start | bytes 6291460
  255.1 3.2 copy-start.2
  258.3 82.5 %all-reduce.5.cloned.1.call-start = ((), (), s32[]{:S(2)}) async-start(), calls=%async_computation.2 | async-start | bytes 524288
Sparse Core Ops, SparseCore 0:
  258.4 26.2 reduce-scatter.2
  288.6 52.1 all-reduce.4
where the time goes:
time: 352 us; the launch traced here: 351 us
  blocking collectives  192 us (55%)
  waiting for transfers between devices  78.2 us (22%)
  matrix products  50.5 us (14%)
  between operations  16.2 us (5%)
  local copies, waits for them, and re-layouts  7.42 us (2%)
  other arithmetic  6.79 us (2%)
    all_gather x1, blocking collectives, shards(): lax.all_gather(packed, ('dp', 'tensor'), axis=0, tiled=True)  70.4 us
    unnamed x3, waiting for transfers between devices  53.1 us
    unnamed x1, blocking collectives  42 us
    psum x1, blocking collectives, shards(): row_total, picked = lax.psum((shifted_total, local_pick), ('dp', 'tensor'))  41.5 us
    pmax x1, blocking collectives, shards(): row_top = lax.pmax(local_top, ('dp', 'tensor'))  37.6 us
    dot_general x1, matrix products, shards(): jnp.einsum('rd,vd->rv', gathered, out_weight, preferred_element_type=jnp....  26 us
    reduce_scatter x1, waiting for transfers between devices, shards(): lax.psum_scatter(grad_term, 'tensor', scatter_dimension=1, tiled=True)  25.1 us
    dot_general x1, matrix products, shards(): jnp.dot(coefficient, out_weight, preferred_element_type=jnp.float32)  24.1 us
  transfers between devices with their start and end apart: 2, of which 2 were waited for; matrix products, arithmetic and copies ran while one was open for 1% of the time, Pallas kernels for 0%

commit v1 on v0

--- a/solution.py
+++ b/solution.py
@@ -1,12 +1,389 @@
+import functools
+
 import jax
 import jax.numpy as jnp
 from jax import lax
+from jax.experimental import pallas as pl
+from jax.experimental.pallas import tpu as pltpu
 from jax.sharding import PartitionSpec as P
 
 CAP = 1
 
 
 loss_scale = 128.0
+
+CORES = 2
+PIECES = 16
+TILE = 256
+RING = 10
+LOW = -1e30
+
+
+def kernel(
+    sizes, kept_ref, mask_ref, target_ref, hidden_ref, weight_ref,
+    grad_ref, loss_ref, pos_ref,
+    rows, ring, gathered, wide, packed, acc, hit_acc,
+    sums, hits, stats,
+    core_sums, core_hits, core_stats,
+    group_out, group_in, group_stats,
+    column_out, column_in, column_stats, column_own,
+    rows_sem, ring_sem, send_sem, recv_sem,
+):
+    chips, depth, vocab_rows, width = sizes
+    half = chips * depth
+    slots = CORES * half
+    piece = width // PIECES
+    tiles = -(-vocab_rows // TILE)
+    tail = vocab_rows - (tiles - 1) * TILE
+    f32, bf16 = jnp.float32, jnp.bfloat16
+
+    dp = lax.axis_index("dp")
+    z = lax.axis_index("tensor")
+    chip = dp // CORES
+    core = dp % CORES
+    slot = core * half + chip * depth + z
+
+    def tile_copy(j):
+        at = lax.rem(j, RING)
+        first = pl.multiple_of((j - 1) * TILE, TILE)
+        return pltpu.make_async_copy(
+            weight_ref.at[pl.ds(first, TILE)], ring.at[at], ring_sem.at[at]
+        )
+
+    tail_copy = pltpu.make_async_copy(
+        weight_ref.at[pl.ds((tiles - 1) * TILE, tail)],
+        ring.at[0, pl.ds(0, tail)],
+        ring_sem.at[0],
+    )
+    rows_copy = pltpu.make_async_copy(hidden_ref, rows, rows_sem)
+    rows_copy.start()
+    if tail < TILE:
+        zero_from = tail // 16 * 16
+        ring[0, zero_from:, :] = jnp.zeros((TILE - zero_from, width), bf16)
+    tail_copy.start()
+    for j in range(1, min(RING, tiles)):
+        tile_copy(j).start()
+
+    chip_peers = [lax.rem(chip + k, chips) for k in range(1, chips)]
+    chip_froms = [lax.rem(chip + chips - k, chips) for k in range(1, chips)]
+    depth_peers = [lax.rem(z + k, depth) for k in range(1, depth)]
+    depth_froms = [lax.rem(z + depth - k, depth) for k in range(1, depth)]
+    other = 1 - core
+
+    def to_depth(peer):
+        return (dp, peer)
+
+    def to_chip(peer):
+        return (peer * CORES + core, z)
+
+    to_core = (chip * CORES + other, z)
+    everyone = [to_depth(p) for p in depth_peers] + [to_chip(p) for p in chip_peers] + [to_core]
+    barrier = pltpu.get_barrier_semaphore()
+    for peer in everyone:
+        pl.semaphore_signal(barrier, inc=1, device_id=peer, device_id_type=pl.DeviceIdType.MESH)
+
+    mask = mask_ref[...]
+    lanes = lax.broadcasted_iota(jnp.int32, mask.shape, 1)
+    count = mask.shape[1]
+    kept = kept_ref[0]
+    first = jnp.min(jnp.where(mask == 1, lanes, count), axis=1, keepdims=True)
+    first = jnp.where(kept > 0, first, count)
+    hit = lanes == first
+    filled = first < count
+    target = jnp.sum(jnp.where(hit, target_ref[...], 0), axis=1, keepdims=True)
+    digits = (
+        jnp.where(filled, target & 255, -1),
+        jnp.where(filled, (target >> 8) & 255, 0),
+        jnp.where(filled, target >> 16, 0),
+    )
+    piece_row = lax.broadcasted_iota(jnp.int32, (PIECES, 128), 0)
+    coded = jnp.zeros((PIECES, 128), jnp.int32)
+    for k, digit in enumerate(digits):
+        coded = jnp.where(piece_row == k, digit, coded)
+    own_rows = pl.ds(pl.multiple_of(slot * PIECES, PIECES), PIECES)
+    gathered[own_rows, piece:] = coded.astype(f32).astype(bf16)
+    select_row = lax.broadcasted_iota(jnp.int32, (PIECES, count), 0)
+    hit_rows = jnp.broadcast_to(hit.astype(f32), (PIECES, count))
+    rows_copy.wait()
+    own = jnp.zeros((PIECES, piece), f32)
+    for a in range(PIECES):
+        chosen = jnp.where(select_row == a, hit_rows, 0.0).astype(bf16)
+        own += jnp.dot(chosen, rows[:, a * piece:(a + 1) * piece], preferred_element_type=f32)
+    gathered[own_rows, :piece] = own.astype(bf16)
+
+    started = []
+    next_sem = [0]
+
+    def send(src, dst, peer):
+        k = next_sem[0]
+        next_sem[0] += 1
+        copy = pltpu.make_async_remote_copy(
+            src_ref=src, dst_ref=dst, send_sem=send_sem.at[k], recv_sem=recv_sem.at[k],
+            device_id=peer, device_id_type=pl.DeviceIdType.MESH,
+        )
+        copy.start()
+        started.append(copy)
+        return copy
+
+    pl.semaphore_wait(barrier, len(everyone))
+    part = gathered.at[own_rows]
+    for copy in [send(part, part, to_depth(p)) for p in depth_peers]:
+        copy.wait_recv()
+    first_row = pl.multiple_of((core * half + chip * depth) * PIECES, PIECES)
+    part = gathered.at[pl.ds(first_row, depth * PIECES)]
+    for copy in [send(part, part, to_chip(p)) for p in chip_peers]:
+        copy.wait_recv()
+    first_row = pl.multiple_of(core * (half * PIECES), PIECES)
+    part = gathered.at[pl.ds(first_row, half * PIECES)]
+    send(part, part, to_core).wait_recv()
+
+    lane_blocks = piece // 128
+    for b in range(lane_blocks + 1):
+        wide[b] = gathered[:, b * 128:(b + 1) * 128].astype(f32)
+    for a in range(PIECES):
+        for b in range(lane_blocks):
+            low = a * piece + b * 128
+            packed[:, low:low + 128] = wide[b, pl.ds(a, slots, stride=PIECES), :].astype(bf16)
+    code = [wide[lane_blocks, pl.ds(k, slots, stride=PIECES), :] for k in range(3)]
+    slot_target = (code[0] + 256.0 * code[1] + 65536.0 * code[2]).astype(jnp.int32)[:, :1]
+    acc[...] = jnp.zeros_like(acc)
+    hit_acc[...] = jnp.zeros_like(hit_acc)
+
+    vocab_first = (dp * depth + z) * vocab_rows
+    columns = lax.broadcasted_iota(jnp.int32, (slots, TILE), 1)
+
+    def logits_of(at):
+        return lax.dot_general(
+            packed[...], ring[at], (((1,), (1,)), ((), ())), preferred_element_type=f32
+        )
+
+    def absorb(j, logits, top, total, picked):
+        at = lax.rem(j, RING)
+        begin = jnp.where(j == 0, tiles - 1, j - 1) * TILE
+        size = jnp.where(j == 0, tail, TILE)
+        valid = columns < size
+        logits = jnp.where(valid, logits, LOW)
+        here = valid & (columns + (vocab_first + begin) == slot_target)
+        later_top = jnp.maximum(top, jnp.max(logits, axis=1, keepdims=True))
+        fade = jnp.exp(top - later_top)
+        weights = jnp.exp(logits - later_top)
+        total = total * fade + jnp.sum(weights, axis=1, keepdims=True)
+        picked = picked + jnp.sum(jnp.where(here, logits, 0.0), axis=1, keepdims=True)
+        both = jnp.concatenate(
+            [jnp.where(here, 0.0, weights), here.astype(f32)], axis=0
+        ).astype(bf16)
+        for a in range(PIECES):
+            cut = slice(a * piece, (a + 1) * piece)
+            term = jnp.dot(both, ring[at, :, cut], preferred_element_type=f32)
+            acc[:, cut] = acc[:, cut] * fade + term[:slots]
+            hit_acc[:, cut] += term[slots:]
+        return later_top, total, picked
+
+    def step(j, carry):
+        logits, top, total, picked = carry
+        tile_copy(j + 1).wait()
+        later = logits_of(lax.rem(j + 1, RING))
+        top, total, picked = absorb(j, logits, top, total, picked)
+
+        @pl.when(j + RING < tiles)
+        def _():
+            tile_copy(j + RING).start()
+
+        return later, top, total, picked
+
+    tail_copy.wait()
+    start = jnp.zeros((slots, 1), f32)
+    carry = (logits_of(0), start + LOW, start, start)
+    carry = lax.fori_loop(0, tiles - 1, step, carry)
+    top, total, picked = absorb(jnp.int32(tiles - 1), *carry)
+
+    def by_slot(source):
+        for a in range(PIECES):
+            for b in range(lane_blocks):
+                low = a * piece + b * 128
+                wide[b, pl.ds(a, slots, stride=PIECES), :] = source[:, low:low + 128]
+
+    by_slot(acc)
+    for b in range(lane_blocks):
+        sums[:, b * 128:(b + 1) * 128] = wide[b]
+    by_slot(hit_acc)
+    for b in range(lane_blocks):
+        hits[:, b * 128:(b + 1) * 128] = wide[b].astype(bf16)
+    stats[...] = jnp.zeros_like(stats)
+    for k, value in enumerate((top, total, picked)):
+        stats[pl.ds(k, slots, stride=8), :] = jnp.broadcast_to(value, (slots, 128))
+
+    def merge(parts):
+        tops = [s[0:1] for _, _, s in parts]
+        top = functools.reduce(jnp.maximum, tops)
+        fades = [jnp.exp(t - top) for t in tops]
+        total = sum(f * s[1:2] for f, (_, _, s) in zip(fades, parts))
+        picked = sum(s[2:3] for _, _, s in parts)
+        grad = sum(
+            jnp.concatenate([f] * lane_blocks, axis=1) * g for f, (g, _, _) in zip(fades, parts)
+        )
+        target_row = sum(h for _, h, _ in parts)
+        return grad, target_row, top, total, picked
+
+    def block_of(top, total, picked):
+        row = lax.broadcasted_iota(jnp.int32, (8, 128), 0)
+        zero = jnp.zeros((8, 128), f32)
+        return jnp.where(row == 0, top, jnp.where(row == 1, total, jnp.where(row == 2, picked, zero)))
+
+    theirs = pl.multiple_of(other * (half * PIECES), PIECES)
+    their_stats = pl.multiple_of(other * (half * 8), 8)
+    copies = [
+        send(stats.at[pl.ds(their_stats, half * 8)], core_stats, to_core),
+        send(sums.at[pl.ds(theirs, half * PIECES)], core_sums, to_core),
+        send(hits.at[pl.ds(theirs, half * PIECES)], core_hits, to_core),
+    ]
+    for copy in copies:
+        copy.wait_recv()
+    mine = pl.multiple_of(core * (half * PIECES), PIECES)
+    mine_stats = pl.multiple_of(core * (half * 8), 8)
+
+    def core_merge(s, _):
+        at = pl.ds(pl.multiple_of(mine + s * PIECES, PIECES), PIECES)
+        at_stats = pl.ds(pl.multiple_of(mine_stats + s * 8, 8), 8)
+        there = pl.ds(pl.multiple_of(s * PIECES, PIECES), PIECES)
+        there_stats = pl.ds(pl.multiple_of(s * 8, 8), 8)
+        grad, target_row, *rest = merge([
+            (sums[at], hits[at].astype(f32), stats[at_stats]),
+            (core_sums[there], core_hits[there].astype(f32), core_stats[there_stats]),
+        ])
+        core_sums[there] = grad
+        core_stats[there_stats] = block_of(*rest)
+        lower = pl.multiple_of(s * (2 * PIECES), PIECES)
+        group_out[pl.ds(lower, PIECES)] = grad.astype(bf16)
+        group_out[pl.ds(lower + PIECES, PIECES)] = target_row.astype(bf16)
+        return 0
+
+    lax.fori_loop(0, half, core_merge, 0, unroll=4)
+
+    span = depth * 2 * PIECES
+    copies = []
+    for k, peer in enumerate(chip_peers):
+        copies.append(send(
+            core_stats.at[pl.ds(pl.multiple_of(peer * (depth * 8), 8), depth * 8)],
+            group_stats.at[k], to_chip(peer),
+        ))
+        copies.append(send(
+            group_out.at[pl.ds(pl.multiple_of(peer * span, PIECES), span)],
+            group_in.at[k], to_chip(peer),
+        ))
+    for copy in copies:
+        copy.wait_recv()
+    for s in range(depth):
+        at = pl.ds(pl.multiple_of((chip * depth + s) * PIECES, PIECES), PIECES)
+        at_stats = pl.ds(pl.multiple_of((chip * depth + s) * 8, 8), 8)
+        own_hit = pl.ds(pl.multiple_of((chip * depth + s) * (2 * PIECES) + PIECES, PIECES), PIECES)
+        low = s * 2 * PIECES
+        parts = [(core_sums[at], group_out[own_hit].astype(f32), core_stats[at_stats])]
+        for k in range(chips - 1):
+            parts.append((
+                group_in[k, low:low + PIECES].astype(f32),
+                group_in[k, low + PIECES:low + 2 * PIECES].astype(f32),
+                group_stats[k, s * 8:s * 8 + 8],
+            ))
+        grad, target_row, *rest = merge(parts)
+        core_sums[at] = grad
+        column_own[s * 8:s * 8 + 8] = block_of(*rest)
+        column_out[low:low + PIECES] = grad.astype(bf16)
+        column_out[low + PIECES:low + 2 * PIECES] = target_row.astype(bf16)
+
+    copies = []
+    for k, peer in enumerate(depth_peers):
+        copies.append(send(
+            column_own.at[pl.ds(pl.multiple_of(peer * 8, 8), 8)], column_stats.at[k], to_depth(peer)
+        ))
+        copies.append(send(
+            column_out.at[pl.ds(pl.multiple_of(peer * (2 * PIECES), PIECES), 2 * PIECES)],
+            column_in.at[k], to_depth(peer),
+        ))
+    for copy in copies:
+        copy.wait_recv()
+    parts = [(
+        core_sums[pl.ds(pl.multiple_of((chip * depth + z) * PIECES, PIECES), PIECES)],
+        column_out[pl.ds(pl.multiple_of(z * (2 * PIECES) + PIECES, PIECES), PIECES)].astype(f32),
+        column_own[pl.ds(pl.multiple_of(z * 8, 8), 8)],
+    )]
+    for k in range(depth - 1):
+        parts.append((
+            column_in[k, :PIECES].astype(f32), column_in[k, PIECES:].astype(f32), column_stats[k]
+        ))
+    grad, target_row, top, total, picked = merge(parts)
+    log_total = top + jnp.log(total)
+    share = jnp.concatenate([1.0 / total] * lane_blocks, axis=1)
+    at_target = (jnp.exp(picked - log_total) - 1.0).astype(bf16).astype(f32)
+    at_target = jnp.concatenate([at_target] * lane_blocks, axis=1)
+    grad = (grad * share + target_row * at_target) * loss_scale
+    for a in range(PIECES):
+        grad_ref[:, a * piece:(a + 1) * piece] = grad[a:a + 1]
+    loss_ref[...] = jnp.where(hit, (log_total - picked)[:, :1], 0.0)
+    pos_ref[...] = jnp.broadcast_to(first, pos_ref.shape)
+    for copy in started:
+        copy.wait_send()
+
+
+def fused_shards(hidden, out_weight, loss_mask, targets, kept_count):
+    count, width = hidden.shape
+    vocab_rows = out_weight.shape[0]
+    chips = lax.axis_size("dp") // CORES
+    depth = lax.axis_size("tensor")
+    half = chips * depth
+    slots = CORES * half
+    piece = width // PIECES
+    f32, bf16 = jnp.float32, jnp.bfloat16
+    copies = 2 * (depth - 1) + 2 * (chips - 1) + (chips - 1) + (depth - 1) + 4
+    vmem, any_space = pl.BlockSpec(memory_space=pltpu.VMEM), pl.BlockSpec(memory_space=pl.ANY)
+    row_grad, row_loss, pos = pl.pallas_call(
+        functools.partial(kernel, (chips, depth, vocab_rows, width)),
+        out_shape=(
+            jax.ShapeDtypeStruct((1, width), f32),
+            jax.ShapeDtypeStruct((1, count), f32),
+            jax.ShapeDtypeStruct((1, count), jnp.int32),
+        ),
+        in_specs=[pl.BlockSpec(memory_space=pltpu.SMEM), vmem, vmem, any_space, any_space],
+        out_specs=(vmem, vmem, vmem),
+        scratch_shapes=[
+            pltpu.VMEM((count, width), bf16),
+            pltpu.VMEM((RING, TILE, width), bf16),
+            pltpu.VMEM((slots * PIECES, piece + 128), bf16),
+            pltpu.VMEM((piece // 128 + 1, slots * PIECES, 128), f32),
+            pltpu.VMEM((slots, width), bf16),
+            pltpu.VMEM((slots, width), f32),
+            pltpu.VMEM((slots, width), f32),
+            pltpu.VMEM((slots * PIECES, piece), f32),
+            pltpu.VMEM((slots * PIECES, piece), bf16),
+            pltpu.VMEM((slots * 8, 128), f32),
+            pltpu.VMEM((half * PIECES, piece), f32),
+            pltpu.VMEM((half * PIECES, piece), bf16),
+            pltpu.VMEM((half * 8, 128), f32),
+            pltpu.VMEM((half * 2 * PIECES, piece), bf16),
+            pltpu.VMEM((chips - 1, depth * 2 * PIECES, piece), bf16),
+            pltpu.VMEM((chips - 1, depth * 8, 128), f32),
+            pltpu.VMEM((depth * 2 * PIECES, piece), bf16),
+            pltpu.VMEM((depth - 1, 2 * PIECES, piece), bf16),
+            pltpu.VMEM((depth - 1, 8, 128), f32),
+            pltpu.VMEM((depth * 8, 128), f32),
+            pltpu.SemaphoreType.DMA,
+            pltpu.SemaphoreType.DMA((RING,)),
+            pltpu.SemaphoreType.DMA((copies,)),
+            pltpu.SemaphoreType.DMA((copies,)),
+        ],
+        compiler_params=pltpu.CompilerParams(
+            collective_id=0, has_side_effects=True, vmem_limit_bytes=60 * 2**20
+        ),
+        cost_estimate=pl.CostEstimate(
+            flops=6 * slots * vocab_rows * width,
+            bytes_accessed=2 * (vocab_rows + count) * width,
+            transcendentals=slots * vocab_rows,
+        ),
+        name="loss_and_gradient",
+    )(kept_count, loss_mask.reshape(1, count), targets.reshape(1, count), hidden, out_weight)
+    chosen = lax.broadcasted_iota(jnp.int32, (count, 1), 0) == pos[0, 0]
+    hidden_grad = jnp.where(chosen, row_grad, 0.0).astype(jnp.bfloat16)
+    return hidden_grad, row_loss.reshape(count)
 
 
 def shards(hidden, out_weight, loss_mask, targets, kept_count):
@@ -55,6 +432,21 @@
     return (hidden_grad, row_loss)
 
 
+def fits(mesh, hidden, out_weight):
+    devices = mesh.shape["dp"] * mesh.shape["tensor"]
+    return (
+        mesh.shape["dp"] % CORES == 0
+        and mesh.shape["dp"] > CORES
+        and mesh.shape["tensor"] > 1
+        and devices <= 32
+        and hidden.shape[1] <= 8192
+        and hidden.shape[1] % (PIECES * 128) == 0
+        and out_weight.shape[0] < 2**24
+        and out_weight.shape[0] % (devices * 8) == 0
+        and out_weight.shape[0] // devices > TILE
+    )
+
+
 def solution(mesh):
     in_specs = (
         P(("dp", "tensor"), None),
@@ -64,4 +456,12 @@
         P(("dp", "tensor")),
     )
     out_specs = (P(("dp", "tensor"), None), P(("dp", "tensor")))
-    return jax.shard_map(shards, mesh=mesh, in_specs=in_specs, out_specs=out_specs, check_vma=False)
+
+    def run(hidden, out_weight, loss_mask, targets, kept_count):
+        body = fused_shards if fits(mesh, hidden, out_weight) else shards
+        mapped = jax.shard_map(
+            body, mesh=mesh, in_specs=in_specs, out_specs=out_specs, check_vma=False
+        )
+        return mapped(hidden, out_weight, loss_mask, targets, kept_count)
+
+    return run

time: 352 us -> 80.6 us (0.23)
  blocking collectives: 192 us -> 0 us
  waiting for transfers between devices: 78.2 us -> 0 us
  Pallas kernels: 0 us -> 75.5 us
  matrix products: 50.5 us -> 0 us
  between operations: 16.2 us -> 1.3 us
  local copies, waits for them, and re-layouts: 7.42 us -> 0.52 us
  other arithmetic: 6.79 us -> 3.04 us
    pallas_call x0 -> x1, Pallas kernels: none -> 75.5 us  [fused_shards(): pl.pallas_call(functools.partial(kernel, (chips, depth, vocab_rows, width...]
    all_gather x1 -> x0, blocking collectives: 70.4 us -> none  [shards(): lax.all_gather(packed, ('dp', 'tensor'), axis=0, tiled=True)]
    unnamed x3 -> x0, waiting for transfers between devices: 53.1 us -> none
    dot_general x3 -> x0, matrix products: 50.5 us -> none  [the longest x1 26 us: shards(): jnp.einsum('rd,vd->rv', gathered, out_weight, preferred_element_type=jnp....]
    unnamed x1 -> x0, blocking collectives: 42 us -> none
    psum x1 -> x0, blocking collectives: 41.5 us -> none  [shards(): row_total, picked = lax.psum((shifted_total, local_pick), ('dp', 'tensor'))]
    pmax x1 -> x0, blocking collectives: 37.6 us -> none  [shards(): row_top = lax.pmax(local_top, ('dp', 'tensor'))]
    reduce_scatter x1 -> x0, waiting for transfers between devices: 25.1 us -> none  [shards(): lax.psum_scatter(grad_term, 'tensor', scatter_dimension=1, tiled=True)]
  transfers between devices with their start and end apart: 2 -> 0, of which waited for: 2 -> 0; matrix products, arithmetic and copies ran while one was open for 1% -> 0% of each run, Pallas kernels for 0% -> 0%
where the time goes in v1:
time: 80.6 us; the launch traced here: 80.4 us
  Pallas kernels  75.5 us (94%)
  other arithmetic  3.04 us (4%)
  between operations  1.3 us (2%)
    pallas_call x1, Pallas kernels, fused_shards(): pl.pallas_call(functools.partial(kernel, (chips, depth, vocab_rows, width...  75.5 us
    convert_element_type x1, other arithmetic, fused_shards(): hidden_grad = jnp.where(chosen, row_grad, 0.0).astype(jnp.bfloat16)  2.42 us

profile of v1, /device:TPU:0, one launch (start us, length us, event | category | flops | bytes accessed | tf_op | source)
XLA Modules:
  0.0 80.4 jit_solution(10036314671136352882)
XLA Ops:
  1.3 75.5 %loss_and_gradient.1 = (f32[1,8192]{1,0:T(1,128)}, f32[1,128]{1,0:T(1,128)}, s32[1,128]{1,0:T(1,128)}) custom-call(s32[1]{0:T(128)S(6)} %copy.8.kept_ref, s32[1,128]{1,0:T(1,128)} %bitcast.7, s32[1,128]{1,0:T(1,128)} %bitcast.8, bf16[128,8192]{1,0:T(8,128)(2,1)} %hidden_ref.1, bf16[4008,8192]{1,0:T(8,128)(2,1)} %weight_ref.1), custom_call_target="tpu_custom_call" | custom-call | flops 6304038912 | bytes 67764224 | tf_op jit(solution)/shard_map/loss_and_gradient/pallas_call | solution.py:339
  76.8 0.0 copy-start
  76.8 0.6 iota_compare_fusion
  77.4 2.4 %select_convert_fusion = bf16[128,8192]{1,0:T(8,128)(2,1)} fusion(f32[8192]{0:T(1024)} %bitcast.6, pred[128]{0:T(512)(128)(4,1)S(1)} %iota_compare_fusion), kind=kLoop, calls=%fused_computation | loop fusion | flops 1048576 | bytes 2130048 | tf_op jit(solution)/shard_map/convert_element_type | solution.py:385
  79.8 0.0 copy-done
  79.8 0.5 copy.9
Async XLA Ops:
  76.8 3.1 %copy-start = (f32[1,128]{1,0:T(1,128)S(1)}, f32[1,128]{1,0:T(1,128)}, u32[]{:S(2)}) copy-start(f32[1,128]{1,0:T(1,128)} %get-tuple-element.7) | copy-start | bytes 1540

commit v2 on v1

--- a/solution.py
+++ b/solution.py
@@ -14,8 +14,8 @@
 
 CORES = 2
 PIECES = 16
-TILE = 256
-RING = 10
+TILE = 512
+RING = 5
 LOW = -1e30
 
 
@@ -143,7 +143,7 @@
     for a in range(PIECES):
         for b in range(lane_blocks):
             low = a * piece + b * 128
-            packed[:, low:low + 128] = wide[b, pl.ds(a, slots, stride=PIECES), :].astype(bf16)
+            packed[low:low + 128, :] = wide[b, pl.ds(a, slots, stride=PIECES), :].T.astype(bf16)
     code = [wide[lane_blocks, pl.ds(k, slots, stride=PIECES), :] for k in range(3)]
     slot_target = (code[0] + 256.0 * code[1] + 65536.0 * code[2]).astype(jnp.int32)[:, :1]
     acc[...] = jnp.zeros_like(acc)
@@ -153,9 +153,7 @@
     columns = lax.broadcasted_iota(jnp.int32, (slots, TILE), 1)
 
     def logits_of(at):
-        return lax.dot_general(
-            packed[...], ring[at], (((1,), (1,)), ((), ())), preferred_element_type=f32
-        )
+        return jnp.dot(ring[at], packed[...], preferred_element_type=f32).T
 
     def absorb(j, logits, top, total, picked):
         at = lax.rem(j, RING)
@@ -325,6 +323,13 @@
         copy.wait_send()
 
 
+def spread(grad_ref, loss_ref, pos_ref, hidden_grad_ref, row_loss_ref):
+    rows, lanes = hidden_grad_ref.shape
+    chosen = lax.broadcasted_iota(jnp.int32, (rows, lanes), 0) == pos_ref[:, :1]
+    hidden_grad_ref[...] = jnp.where(chosen, grad_ref[...], 0.0).astype(hidden_grad_ref.dtype)
+    row_loss_ref[...] = loss_ref[0, :]
+
+
 def fused_shards(hidden, out_weight, loss_mask, targets, kept_count):
     count, width = hidden.shape
     vocab_rows = out_weight.shape[0]
@@ -350,7 +355,7 @@
             pltpu.VMEM((RING, TILE, width), bf16),
             pltpu.VMEM((slots * PIECES, piece + 128), bf16),
             pltpu.VMEM((piece // 128 + 1, slots * PIECES, 128), f32),
-            pltpu.VMEM((slots, width), bf16),
+            pltpu.VMEM((width, slots), bf16),
             pltpu.VMEM((slots, width), f32),
             pltpu.VMEM((slots, width), f32),
             pltpu.VMEM((slots * PIECES, piece), f32),
@@ -381,9 +386,24 @@
         ),
         name="loss_and_gradient",
     )(kept_count, loss_mask.reshape(1, count), targets.reshape(1, count), hidden, out_weight)
-    chosen = lax.broadcasted_iota(jnp.int32, (count, 1), 0) == pos[0, 0]
-    hidden_grad = jnp.where(chosen, row_grad, 0.0).astype(jnp.bfloat16)
-    return hidden_grad, row_loss.reshape(count)
+    return pl.pallas_call(
+        spread,
+        out_shape=(
+            jax.ShapeDtypeStruct((count, width), bf16),
+            jax.ShapeDtypeStruct((count,), f32),
+        ),
+        grid=(8,),
+        in_specs=[
+            pl.BlockSpec((1, width // 8), lambda i: (0, i)),
+            pl.BlockSpec((1, count), lambda i: (0, 0)),
+            pl.BlockSpec((1, count), lambda i: (0, 0)),
+        ],
+        out_specs=(
+            pl.BlockSpec((count, width // 8), lambda i: (0, i)),
+            pl.BlockSpec((count,), lambda i: (0,)),
+        ),
+        name="spread",
+    )(row_grad, row_loss, pos)
 
 
 def shards(hidden, out_weight, loss_mask, targets, kept_count):

time: 80.6 us -> 79.3 us (0.984)
  other arithmetic: 3.04 us -> 0 us
  Pallas kernels: 75.5 us -> 77.7 us
    pallas_call x0 -> x1, Pallas kernels: none -> 4.6 us  [fused_shards(): pl.pallas_call(spread, out_shape=(jax.ShapeDtypeStruct((count, width), bf...]
    convert_element_type x1 -> x0, other arithmetic: 2.42 us -> none  [fused_shards(): hidden_grad = jnp.where(chosen, row_grad, 0.0).astype(jnp.bfloat16)]
    pallas_call x1, Pallas kernels: 75.5 us -> 73.1 us  [fused_shards(): pl.pallas_call(functools.partial(kernel, (chips, depth, vocab_rows, width...]
where the time goes in v2:
time: 79.3 us; the launch traced here: 79 us
  Pallas kernels  77.7 us (98%)
  between operations  1.29 us (2%)
    pallas_call x1, Pallas kernels, fused_shards(): pl.pallas_call(functools.partial(kernel, (chips, depth, vocab_rows, width...  73.1 us
    pallas_call x1, Pallas kernels, fused_shards(): pl.pallas_call(spread, out_shape=(jax.ShapeDtypeStruct((count, width), bf...  4.6 us

profile of v2, /device:TPU:0, one launch (start us, length us, event | category | flops | bytes accessed | tf_op | source)
XLA Modules:
  0.0 79.0 jit_solution(4356087153132284336)
XLA Ops:
  1.3 73.1 %loss_and_gradient.1 = (f32[1,8192]{1,0:T(1,128)}, f32[1,128]{1,0:T(1,128)}, s32[1,128]{1,0:T(1,128)}) custom-call(s32[1]{0:T(128)S(6)} %copy.7.kept_ref, s32[1,128]{1,0:T(1,128)} %bitcast.2, s32[1,128]{1,0:T(1,128)} %bitcast.3, bf16[128,8192]{1,0:T(8,128)(2,1)} %hidden_ref.1, bf16[4008,8192]{1,0:T(8,128)(2,1)} %weight_ref.1), custom_call_target="tpu_custom_call" | custom-call | flops 6304038912 | bytes 67764224 | tf_op jit(solution)/shard_map/loss_and_gradient/pallas_call | solution.py:344
  74.4 4.6 %spread.1 = (bf16[128,8192]{1,0:T(8,128)(2,1)}, f32[128]{0:T(128)}) custom-call(f32[1,8192]{1,0:T(1,128)} %get-tuple-element.5.grad_ref, f32[1,128]{1,0:T(1,128)} %get-tuple-element.6.loss_ref, s32[1,128]{1,0:T(1,128)} %get-tuple-element.7.pos_ref), custom_call_target="tpu_custom_call" | custom-call | tf_op jit(solution)/shard_map/spread/pallas_call | solution.py:389

commit v3 on v1

--- a/solution.py
+++ b/solution.py
@@ -14,8 +14,8 @@
 
 CORES = 2
 PIECES = 16
-TILE = 256
-RING = 10
+TILE = 512
+RING = 5
 LOW = -1e30
 
 
@@ -127,15 +127,23 @@
 
     pl.semaphore_wait(barrier, len(everyone))
     part = gathered.at[own_rows]
-    for copy in [send(part, part, to_depth(p)) for p in depth_peers]:
+    from_column = [send(part, part, to_depth(p)) for p in depth_peers]
+    from_chips = [[send(part, part, to_chip(p))] for p in chip_peers]
+    for copy, source in zip(from_column, depth_froms):
         copy.wait_recv()
-    first_row = pl.multiple_of((core * half + chip * depth) * PIECES, PIECES)
-    part = gathered.at[pl.ds(first_row, depth * PIECES)]
-    for copy in [send(part, part, to_chip(p)) for p in chip_peers]:
+        first_row = pl.multiple_of((core * half + chip * depth + source) * PIECES, PIECES)
+        part = gathered.at[pl.ds(first_row, PIECES)]
+        for copies, peer in zip(from_chips, chip_peers):
+            copies.append(send(part, part, to_chip(peer)))
+    from_core = []
+    for copies, source in zip([[]] + from_chips, [chip] + chip_froms):
+        for copy in copies:
+            copy.wait_recv()
+        first_row = pl.multiple_of((core * half + source * depth) * PIECES, PIECES)
+        part = gathered.at[pl.ds(first_row, depth * PIECES)]
+        from_core.append(send(part, part, to_core))
+    for copy in from_core:
         copy.wait_recv()
-    first_row = pl.multiple_of(core * (half * PIECES), PIECES)
-    part = gathered.at[pl.ds(first_row, half * PIECES)]
-    send(part, part, to_core).wait_recv()
 
     lane_blocks = piece // 128
     for b in range(lane_blocks + 1):
@@ -143,7 +151,7 @@
     for a in range(PIECES):
         for b in range(lane_blocks):
             low = a * piece + b * 128
-            packed[:, low:low + 128] = wide[b, pl.ds(a, slots, stride=PIECES), :].astype(bf16)
+            packed[low:low + 128, :] = wide[b, pl.ds(a, slots, stride=PIECES), :].T.astype(bf16)
     code = [wide[lane_blocks, pl.ds(k, slots, stride=PIECES), :] for k in range(3)]
     slot_target = (code[0] + 256.0 * code[1] + 65536.0 * code[2]).astype(jnp.int32)[:, :1]
     acc[...] = jnp.zeros_like(acc)
@@ -153,9 +161,7 @@
     columns = lax.broadcasted_iota(jnp.int32, (slots, TILE), 1)
 
     def logits_of(at):
-        return lax.dot_general(
-            packed[...], ring[at], (((1,), (1,)), ((), ())), preferred_element_type=f32
-        )
+        return jnp.dot(ring[at], packed[...], preferred_element_type=f32).T
 
     def absorb(j, logits, top, total, picked):
         at = lax.rem(j, RING)
@@ -230,15 +236,18 @@
         zero = jnp.zeros((8, 128), f32)
         return jnp.where(row == 0, top, jnp.where(row == 1, total, jnp.where(row == 2, picked, zero)))
 
-    theirs = pl.multiple_of(other * (half * PIECES), PIECES)
+    group_order = chip_peers + [chip]
+    slot_order = depth_peers + [z]
     their_stats = pl.multiple_of(other * (half * 8), 8)
-    copies = [
-        send(stats.at[pl.ds(their_stats, half * 8)], core_stats, to_core),
-        send(sums.at[pl.ds(theirs, half * PIECES)], core_sums, to_core),
-        send(hits.at[pl.ds(theirs, half * PIECES)], core_hits, to_core),
-    ]
-    for copy in copies:
-        copy.wait_recv()
+    stats_copy = send(stats.at[pl.ds(their_stats, half * 8)], core_stats, to_core)
+    core_copies = []
+    for group in group_order:
+        theirs = pl.multiple_of((other * half + group * depth) * PIECES, PIECES)
+        there = pl.ds(pl.multiple_of(group * (depth * PIECES), PIECES), depth * PIECES)
+        core_copies.append([
+            send(sums.at[pl.ds(theirs, depth * PIECES)], core_sums.at[there], to_core),
+            send(hits.at[pl.ds(theirs, depth * PIECES)], core_hits.at[there], to_core),
+        ])
     mine = pl.multiple_of(core * (half * PIECES), PIECES)
     mine_stats = pl.multiple_of(core * (half * 8), 8)
 
@@ -258,49 +267,62 @@
         group_out[pl.ds(lower + PIECES, PIECES)] = target_row.astype(bf16)
         return 0
 
-    lax.fori_loop(0, half, core_merge, 0, unroll=4)
-
-    span = depth * 2 * PIECES
-    copies = []
+    def group_merge(copies, group):
+        for copy in copies:
+            copy.wait_recv()
+        lax.fori_loop(0, depth, lambda s, c: core_merge(group * depth + s, c), 0, unroll=True)
+
+    stats_copy.wait_recv()
+    chip_stats = []
     for k, peer in enumerate(chip_peers):
-        copies.append(send(
+        group_merge(core_copies[k], peer)
+        chip_stats.append(send(
             core_stats.at[pl.ds(pl.multiple_of(peer * (depth * 8), 8), depth * 8)],
             group_stats.at[k], to_chip(peer),
         ))
-        copies.append(send(
-            group_out.at[pl.ds(pl.multiple_of(peer * span, PIECES), span)],
-            group_in.at[k], to_chip(peer),
-        ))
-    for copy in copies:
+    from_chips = []
+    for s in slot_order:
+        low = pl.multiple_of(s * (2 * PIECES), PIECES)
+        from_chips.append([
+            send(
+                group_out.at[pl.ds(
+                    pl.multiple_of((peer * depth + s) * (2 * PIECES), PIECES), 2 * PIECES
+                )],
+                group_in.at[k, pl.ds(low, 2 * PIECES)], to_chip(peer),
+            )
+            for k, peer in enumerate(chip_peers)
+        ])
+    group_merge(core_copies[-1], chip)
+    for copy in chip_stats:
         copy.wait_recv()
-    for s in range(depth):
+
+    column_copies = []
+    for n, s in enumerate(slot_order):
+        for copy in from_chips[n]:
+            copy.wait_recv()
         at = pl.ds(pl.multiple_of((chip * depth + s) * PIECES, PIECES), PIECES)
         at_stats = pl.ds(pl.multiple_of((chip * depth + s) * 8, 8), 8)
         own_hit = pl.ds(pl.multiple_of((chip * depth + s) * (2 * PIECES) + PIECES, PIECES), PIECES)
-        low = s * 2 * PIECES
+        low = pl.multiple_of(s * (2 * PIECES), PIECES)
+        at_own = pl.ds(pl.multiple_of(s * 8, 8), 8)
         parts = [(core_sums[at], group_out[own_hit].astype(f32), core_stats[at_stats])]
         for k in range(chips - 1):
             parts.append((
-                group_in[k, low:low + PIECES].astype(f32),
-                group_in[k, low + PIECES:low + 2 * PIECES].astype(f32),
-                group_stats[k, s * 8:s * 8 + 8],
+                group_in[k, pl.ds(low, PIECES)].astype(f32),
+                group_in[k, pl.ds(low + PIECES, PIECES)].astype(f32),
+                group_stats[k, at_own],
             ))
         grad, target_row, *rest = merge(parts)
         core_sums[at] = grad
-        column_own[s * 8:s * 8 + 8] = block_of(*rest)
-        column_out[low:low + PIECES] = grad.astype(bf16)
-        column_out[low + PIECES:low + 2 * PIECES] = target_row.astype(bf16)
-
-    copies = []
-    for k, peer in enumerate(depth_peers):
-        copies.append(send(
-            column_own.at[pl.ds(pl.multiple_of(peer * 8, 8), 8)], column_stats.at[k], to_depth(peer)
-        ))
-        copies.append(send(
-            column_out.at[pl.ds(pl.multiple_of(peer * (2 * PIECES), PIECES), 2 * PIECES)],
-            column_in.at[k], to_depth(peer),
-        ))
-    for copy in copies:
+        column_own[at_own] = block_of(*rest)
+        column_out[pl.ds(low, PIECES)] = grad.astype(bf16)
+        column_out[pl.ds(low + PIECES, PIECES)] = target_row.astype(bf16)
+        if n < depth - 1:
+            column_copies.append(send(column_own.at[at_own], column_stats.at[n], to_depth(s)))
+            column_copies.append(send(
+                column_out.at[pl.ds(low, 2 * PIECES)], column_in.at[n], to_depth(s)
+            ))
+    for copy in column_copies:
         copy.wait_recv()
     parts = [(
         core_sums[pl.ds(pl.multiple_of((chip * depth + z) * PIECES, PIECES), PIECES)],
@@ -334,7 +356,7 @@
     slots = CORES * half
     piece = width // PIECES
     f32, bf16 = jnp.float32, jnp.bfloat16
-    copies = 2 * (depth - 1) + 2 * (chips - 1) + (chips - 1) + (depth - 1) + 4
+    copies = 3 * (depth - 1) + (chips - 1) * (2 * depth + 1) + 3 * chips + 1
     vmem, any_space = pl.BlockSpec(memory_space=pltpu.VMEM), pl.BlockSpec(memory_space=pl.ANY)
     row_grad, row_loss, pos = pl.pallas_call(
         functools.partial(kernel, (chips, depth, vocab_rows, width)),
@@ -350,7 +372,7 @@
             pltpu.VMEM((RING, TILE, width), bf16),
             pltpu.VMEM((slots * PIECES, piece + 128), bf16),
             pltpu.VMEM((piece // 128 + 1, slots * PIECES, 128), f32),
-            pltpu.VMEM((slots, width), bf16),
+            pltpu.VMEM((width, slots), bf16),
             pltpu.VMEM((slots, width), f32),
             pltpu.VMEM((slots, width), f32),
             pltpu.VMEM((slots * PIECES, piece), f32),
@@ -382,7 +404,7 @@
         name="loss_and_gradient",
     )(kept_count, loss_mask.reshape(1, count), targets.reshape(1, count), hidden, out_weight)
     chosen = lax.broadcasted_iota(jnp.int32, (count, 1), 0) == pos[0, 0]
-    hidden_grad = jnp.where(chosen, row_grad, 0.0).astype(jnp.bfloat16)
+    hidden_grad = jnp.where(chosen, row_grad, 0.0).astype(bf16)
     return hidden_grad, row_loss.reshape(count)
 
 

time: 80.6 us -> 74.9 us (0.929)
  Pallas kernels: 75.5 us -> 69.8 us
    pallas_call x1, Pallas kernels: 75.5 us -> 69.8 us  [fused_shards(): pl.pallas_call(functools.partial(kernel, (chips, depth, vocab_rows, width...]
where the time goes in v3:
time: 74.9 us; the launch traced here: 74.7 us
  Pallas kernels  69.8 us (93%)
  other arithmetic  3.04 us (4%)
  between operations  1.3 us (2%)
    pallas_call x1, Pallas kernels, fused_shards(): pl.pallas_call(functools.partial(kernel, (chips, depth, vocab_rows, width...  69.8 us
    convert_element_type x1, other arithmetic, fused_shards(): hidden_grad = jnp.where(chosen, row_grad, 0.0).astype(bf16)  2.42 us

profile of v3, /device:TPU:0, one launch (start us, length us, event | category | flops | bytes accessed | tf_op | source)
XLA Modules:
  0.0 74.7 jit_solution(10042917658083627638)
XLA Ops:
  1.3 69.8 %loss_and_gradient.1 = (f32[1,8192]{1,0:T(1,128)}, f32[1,128]{1,0:T(1,128)}, s32[1,128]{1,0:T(1,128)}) custom-call(s32[1]{0:T(128)S(6)} %copy.8.kept_ref, s32[1,128]{1,0:T(1,128)} %bitcast.7, s32[1,128]{1,0:T(1,128)} %bitcast.8, bf16[128,8192]{1,0:T(8,128)(2,1)} %hidden_ref.1, bf16[4008,8192]{1,0:T(8,128)(2,1)} %weight_ref.1), custom_call_target="tpu_custom_call" | custom-call | flops 6304038912 | bytes 67764224 | tf_op jit(solution)/shard_map/loss_and_gradient/pallas_call | solution.py:361
  71.1 0.0 copy-start
  71.1 0.6 iota_compare_fusion
  71.8 2.4 %select_convert_fusion = bf16[128,8192]{1,0:T(8,128)(2,1)} fusion(f32[8192]{0:T(1024)} %bitcast.6, pred[128]{0:T(512)(128)(4,1)S(1)} %iota_compare_fusion), kind=kLoop, calls=%fused_computation | loop fusion | flops 1048576 | bytes 2130048 | tf_op jit(solution)/shard_map/convert_element_type | solution.py:407
  74.2 0.0 copy-done
  74.2 0.5 copy.9
Async XLA Ops:
  71.1 3.1 %copy-start = (f32[1,128]{1,0:T(1,128)S(1)}, f32[1,128]{1,0:T(1,128)}, u32[]{:S(2)}) copy-start(f32[1,128]{1,0:T(1,128)} %get-tuple-element.7) | copy-start | bytes 1540
